TPU v7x, 128 devices: a whole 4x4x4 slice. The times are simulated.
128 devices in a mesh: mp: 8 (over z, x_lo), dp: 16 (over x_hi, y, core).
Axes of the slice: x: 4 (x_hi: 2, x_lo: 2; x = x_hi * 2 + x_lo), y: 4, z: 4, core: 2. Of those that a mesh axis runs over, the one named last changes fastest.
Arguments:
- volume: bfloat16 [16, 64, 64, 2048], P('dp', 'mp'), may hold values from -6 to 6
- kernel_a: bfloat16 [3, 3, 3, 32, 64], replicated, may hold values from -0.21875 to 0.21875
- kernel_b: bfloat16 [3, 3, 3, 64, 128], P(None, None, None, 'mp'), may hold values from -0.15625 to 0.15625
- cotangent: bfloat16 [16, 16, 16, 16, 128], P('dp', None, None, None, 'mp'), may hold values from -6 to 6
Outputs:
- features: bfloat16 [16, 16, 16, 16, 128], P('dp', None, None, None, 'mp')
- grad_a: float32 [3, 3, 3, 32, 64], replicated
- grad_b: float32 [3, 3, 3, 64, 128], P(None, None, None, 'mp')
All inputs are finite; a program needn't handle non-finite values.
Results may differ from a plain program's by a relative error of at most 0.0049.
Values may be sent and summed in bfloat16 or wider, within the bound.
A program may use at most 192 MiB of HBM per device.

v0:
```python
import math
import jax
import jax.numpy as jnp
from jax import lax
from jax.sharding import PartitionSpec as P

GRID = 64


def shifted(array, axis, by):
    size = lax.axis_size(axis)
    pairs = [(i, i + by) for i in range(size) if 0 <= i + by < size]
    return lax.ppermute(array, axis, pairs)


def forward_conv(padded, kernel):
    return lax.conv_general_dilated(
        padded,
        kernel,
        (2, 2, 2),
        "VALID",
        dimension_numbers=("NDHWC", "DHWIO", "NDHWC"),
        preferred_element_type=jnp.float32,
    )


def kernel_grad(padded, grads):
    result = lax.conv_general_dilated(
        padded,
        grads,
        (1, 1, 1),
        "VALID",
        rhs_dilation=(2, 2, 2),
        dimension_numbers=("CDHWN", "IDHWO", "NDHWC"),
        preferred_element_type=jnp.float32,
    )
    return jnp.transpose(result, (1, 2, 3, 0, 4))


def input_grad(grads, kernel, first_low):
    flipped = kernel[::-1, ::-1, ::-1]
    return lax.conv_general_dilated(
        grads,
        flipped,
        (1, 1, 1),
        ((first_low, 2), (1, 2), (1, 2)),
        lhs_dilation=(2, 2, 2),
        dimension_numbers=("NDHWC", "DHWOI", "NDHWC"),
        preferred_element_type=jnp.float32,
    )


def pad_sides(field):
    return jnp.pad(field, ((0, 0), (0, 0), (1, 0), (1, 0), (0, 0)))


def pad_low(field):
    return jnp.pad(field, ((0, 0), (1, 0), (1, 0), (1, 0), (0, 0)))


def shards(volume, kernel_a, kernel_b, cotangent):
    samp_local = volume.shape[0]
    planes = volume.shape[1]
    edge = volume.shape[2]
    in_chan = kernel_a.shape[3]
    field = volume.reshape(samp_local, planes, edge, edge, in_chan)
    below = shifted(field[:, planes - 1 :], "mp", 1)
    padded_x = pad_sides(jnp.concatenate([below, field], axis=1))
    pre = forward_conv(padded_x, kernel_a)
    hidden = jnp.where(pre > 0, pre, 0.3 * pre).astype(jnp.bfloat16)
    grouped = lax.all_to_all(hidden, "mp", split_axis=4, concat_axis=1, tiled=True)
    padded_h = pad_low(grouped)
    partial_out = forward_conv(padded_h, kernel_b)
    features = lax.psum_scatter(partial_out, "mp", scatter_dimension=4, tiled=True).astype(
        jnp.bfloat16
    )
    upstream = lax.all_gather(cotangent, "mp", axis=4, tiled=True)
    local_b = kernel_grad(padded_h, upstream)
    back_group = input_grad(upstream, kernel_b, 1).astype(jnp.bfloat16)
    back = lax.all_to_all(back_group, "mp", split_axis=1, concat_axis=4, tiled=True)
    delta = (back.astype(jnp.float32) * jnp.where(pre > 0, 1.0, 0.3)).astype(jnp.bfloat16)
    local_a = kernel_grad(padded_x, delta)
    total_a = lax.psum(local_a, ("mp", "dp"))
    total_b = lax.psum(local_b, "dp")
    samples_all = samp_local * lax.axis_size("dp")
    grad_a = total_a / math.sqrt(samples_all * (GRID // 2) ** 3)
    grad_b = total_b / math.sqrt(samples_all * (GRID // 4) ** 3)
    return (features, grad_a, grad_b)


def solution(mesh):
    return jax.shard_map(
        shards,
        mesh=mesh,
        in_specs=(
            P("dp", "mp", None, None),
            P(),
            P(None, None, None, "mp", None),
            P("dp", None, None, None, "mp"),
        ),
        out_specs=(P("dp", None, None, None, "mp"), P(), P(None, None, None, "mp", None)),
        check_vma=False,
    )
```

profile of v0, /device:TPU:1, one launch (start us, length us, event | category | flops | bytes accessed | tf_op | source)
XLA Modules:
  0.0 838.3 jit_solution(7763710412680146833)
XLA Ops:
  7.2 4.9 copy.124
  14.2 4.0 collective-permute-start
  18.2 31.5 %copy.127 = bf16[1,8,64,64,32]{4,0,3,2,1:T(2,128)(2,1)} copy(bf16[1,8,64,64,32]{2,4,3,1,0:T(8,128)(2,1)} %bitcast.69) | data formatting | bytes 4194304 | tf_op jit(solution)/shard_map/reshape | solution.py:66
  49.7 2.7 copy.126
  52.4 58.2 %pad_maximum_fusion = bf16[1,9,64,64,32]{4,0,3,2,1:T(2,128)(2,1)} fusion(bf16[1,8,64,64,32]{4,0,3,2,1:T(2,128)(2,1)} %copy.127, bf16[1,1,64,64,32]{4,0,3,2,1:T(2,128)(2,1)S(1)} %copy.126), kind=kLoop, calls=%fused_computation.4 | loop fusion | flops 1179648 | bytes 4718592 | tf_op jit(solution)/shard_map/concatenate | solution.py:68
  110.6 33.5 %copy.128 = bf16[1,9,64,64,32]{3,4,2,1,0:T(8,128)(2,1)} copy(bf16[1,9,64,64,32]{4,0,3,2,1:T(2,128)(2,1)} %pad_maximum_fusion) | data formatting | bytes 4718592 | tf_op jit(solution)/shard_map/concatenate | solution.py:68
  144.1 9.2 %copy.159 = bf16[9,64,1,64,32]{1,4,3,0,2:T(8,128)(2,1)} copy(bf16[9,64,1,64,32]{3,4,2,1,0:T(8,128)(2,1)} %bitcast.72) | data formatting | bytes 4718592
  153.3 6.1 pad.4.clone
  159.4 15.6 %copy.131 = bf16[9,64,1,8,10,32]{5,3,4,1,0,2:T(8,128)(2,1)} copy(bf16[9,64,1,8,10,32]{1,5,4,3,0,2:T(8,128)(2,1)} %bitcast.67) | data formatting | bytes 5898240 | tf_op jit(solution)/shard_map/conv_general_dilated | solution.py:17
  175.1 2.3 slice.12
  177.4 12.0 %compare_select_fusion = (f32[4,32,8,5,64]{4,2,3,1,0:T(8,128)}, bf16[4,32,8,5,64]{4,2,3,1,0:T(8,128)(2,1)S(1)}) fusion(pred[8,5]{0,1:T(8,128)(4,1)S(1)} %copy-done.6, bf16[3,3,3,32,64]{4,3,2,1,0:T(8,128)(2,1)S(1)} %copy-done, bf16[9,64,1,7,2,32]{5,3,4,1,0,2:T(8,128)(2,1)S(1)} %slice.12, bf16[9,64,1,8,10,32]{5,3,4,1,0,2:T(8,128)(2,1)} %copy.131), kind=kOutput, calls=%fused_computation.20 | convolution fusion | flops 572915712 | bytes 5541928 | tf_op jit(solution)/shard_map/conv_general_dilated | solution.py:17
  189.8 3.2 copy.133
  193.1 2.7 reshape.71
  195.8 6.1 all-to-all-start
  202.0 3.9 copy.140
  206.6 2.8 copy.158
  209.4 1.5 all-to-all-done
  211.9 2.9 copy.134
  214.8 2.2 copy.135
  216.9 3.4 copy.160
  220.4 4.0 pad.6.clone
  224.4 12.8 %copy.138 = bf16[32,32,1,8,6,8]{5,3,4,1,0,2:T(8,128)(2,1)} copy(bf16[32,32,1,8,6,8]{1,5,4,3,0,2:T(8,128)(2,1)} %bitcast.73) | data formatting | bytes 1572864 | tf_op jit(solution)/shard_map/conv_general_dilated | solution.py:17
  237.2 3.4 slice.14
  240.6 12.3 %broadcast_select_fusion = f32[16,16,8,3,128]{4,2,3,1,0:T(8,128)S(1)} fusion(pred[8,3]{0,1:T(4,128)(4,1)S(1)} %copy-done.7, bf16[3,3,3,8,128]{4,3,2,1,0:T(8,128)(2,1)S(1)} %copy-done.5, bf16[32,32,1,7,2,8]{5,3,4,1,0,2:T(8,128)(2,1)S(1)} %slice.14, bf16[32,32,1,8,6,8]{5,3,4,1,0,2:T(8,128)(2,1)} %copy.138), kind=kOutput, calls=%fused_computation.30 | convolution fusion | flops 329662464 | bytes 4216856 | tf_op jit(solution)/shard_map/conv_general_dilated | solution.py:17
  252.9 2.3 copy.139
  255.2 23.8 %copy.153 = bf16[1,32,32,32,8]{4,0,3,2,1:T(2,128)(2,1)} copy(bf16[1,32,32,32,8]{3,4,2,1,0:T(8,128)(2,1)S(1)} %bitcast.71) | data formatting | bytes 1048576 | tf_op jit(solution)/shard_map/all_to_all | solution.py:71
  279.0 97.7 %all-gather.2.cloned.1.call-done = bf16[1,16,16,16,128]{3,2,1,0,4:T(8,128)(2,1)} async-done(((bf16[1,16,16,16,16]{3,2,1,0,4:T(8,128)(2,1)}), bf16[1,16,16,16,128]{3,2,1,0,4:T(8,128)(2,1)}) %all-gather.2.cloned.1.call-update) | async-done | bytes 1048592 | tf_op jit(solution)/shard_map/all_gather | solution.py:77
  376.7 10.0 %copy.141 = bf16[1,16,16,16,128]{4,3,2,1,0:T(8,128)(2,1)S(1)} copy(bf16[1,16,16,16,128]{3,2,1,0,4:T(8,128)(2,1)} %all-gather.2.cloned.1.call-done) | data formatting | bytes 2097152 | tf_op jit(solution)/shard_map/all_gather | solution.py:77
  387.9 14.3 %fusion.17 = bf16[32,32,8,6,8]{4,2,3,1,0:T(8,128)(2,1)} fusion(bf16[3,3,3,8,128]{4,3,2,1,0:T(8,128)(2,1)S(1)} %copy-done.5, bf16[16,16,1,7,1,128]{5,3,4,1,0,2:T(8,128)(2,1)S(1)} %slice.16, bf16[16,16,1,8,3,128]{5,3,4,1,0,2:T(8,128)(2,1)S(1)} %copy.144), kind=kOutput, calls=%fused_computation.24 | convolution fusion | flops 332021760 | bytes 2873344 | tf_op jit(solution)/shard_map/conv_general_dilated | solution.py:42
  402.2 13.6 %copy.145 = bf16[32,32,8,6,8]{1,4,3,2,0:T(8,128)(2,1)S(1)} copy(bf16[32,32,8,6,8]{4,2,3,1,0:T(8,128)(2,1)} %fusion.17) | data formatting | bytes 1572864 | tf_op jit(solution)/shard_map/conv_general_dilated | solution.py:42
  417.0 2.7 reshape.73
  419.7 4.9 all-to-all-start.1
  424.6 13.5 %copy.154 = bf16[1,16,16,16,128]{4,0,3,2,1:T(2,128)(2,1)S(1)} copy(bf16[1,16,16,16,128]{3,2,1,0,4:T(8,128)(2,1)} %all-gather.2.cloned.1.call-done) | data formatting | bytes 2097152 | tf_op jit(solution)/shard_map/all_gather | solution.py:77
  438.1 51.8 %fusion.36 = f32[3,3,3,8,128]{4,3,2,1,0:T(8,128)} fusion(bf16[1,32,32,32,8]{4,0,3,2,1:T(2,128)(2,1)} %copy.153, bf16[1,16,16,16,128]{4,0,3,2,1:T(2,128)(2,1)S(1)} %copy.154), kind=kOutput, calls=%fused_computation.46 | convolution fusion | flops 212629504 | bytes 1683456 | tf_op jit(solution)/shard_map/transpose | solution.py:37
  490.0 1.3 reshape.74
  491.3 3.4 copy.147
  494.7 3.5 fusion.12
  498.2 4.1 copy.151
  502.3 46.6 %fusion.35 = f32[3,3,3,32,64]{4,3,2,1,0:T(8,128)} fusion(bf16[1,9,64,64,32]{4,0,3,2,1:T(2,128)(2,1)} %pad_maximum_fusion, bf16[1,4,32,32,64]{4,0,3,2,1:T(2,128)(2,1)} %copy.151), kind=kOutput, calls=%fused_computation.45 | convolution fusion | flops 443596800 | bytes 3104768 | tf_op jit(solution)/shard_map/transpose | solution.py:37
  548.9 1.6 slice_bitcast_fusion.1
  550.5 14.3 %copy.156 = f32[1,16,16,16,128]{2,3,1,0,4:T(8,128)} copy(f32[1,16,16,16,128]{4,2,3,1,0:T(8,128)} %slice_bitcast_fusion.1) | data formatting | bytes 4194304
  564.8 15.3 %reshape.69 = f32[128,4096]{1,0:T(8,128)} reshape(f32[128,1,16,16,16]{4,3,2,1,0:T(8,128)} %bitcast.66) | data formatting | bytes 4194304
  580.1 45.1 %all-reduce.5.cloned.1.call-done = f32[3,3,3,8,128]{4,3,2,1,0:T(8,128)} async-done(((f32[3,3,3,8,128]{4,3,2,1,0:T(8,128)}), f32[3,3,3,8,128]{4,3,2,1,0:T(8,128)}) %all-reduce.5.cloned.1.call-update) | async-done | bytes 110608 | tf_op jit(solution)/shard_map/psum | solution.py:84
  625.2 1.6 broadcast_multiply_fusion.1
  626.8 147.3 %all-reduce.3.cloned.1.call-done = f32[3,3,3,32,64]{4,3,2,1,0:T(8,128)} async-done(((f32[3,3,3,32,64]{4,3,2,1,0:T(8,128)}), f32[3,3,3,32,64]{4,3,2,1,0:T(8,128)}) %all-reduce.3.cloned.1.call-update) | async-done | bytes 221200 | tf_op jit(solution)/shard_map/psum | solution.py:83
  774.1 1.8 broadcast_multiply_fusion
  775.9 51.3 %reduce-scatter.4.cloned.1.call-done = f32[16,4096]{1,0:T(8,128)} async-done(((f32[128,4096]{1,0:T(8,128)}), f32[16,4096]{1,0:T(8,128)}) %reduce-scatter.4.cloned.1.call-update) | async-done | bytes 262160
  827.2 1.7 reshape.70
  (41 shorter events, 9.2 us)
Async XLA Ops:
  7.2 170.2 %copy-start = (bf16[3,3,3,32,64]{4,3,2,1,0:T(8,128)(2,1)S(1)}, bf16[3,3,3,32,64]{4,3,2,1,0:T(8,128)(2,1)}, u32[]{:S(2)}) copy-start(bf16[3,3,3,32,64]{4,3,2,1,0:T(8,128)(2,1)} %param.5) | copy-start | bytes 331780
  14.2 35.5 %collective-permute-start = (bf16[1,1,64,64,32]{3,4,2,1,0:T(8,128)(2,1)S(1)}, bf16[1,1,64,64,32]{3,4,2,1,0:T(8,128)(2,1)S(1)}, u32[]{:S(2)}, u32[]{:S(2)}) collective-permute-start(bf16[1,1,64,64,32]{3,4,2,1,0:T(8,128)(2,1)S(1)} %copy.125), channel_id=1, source_target_pairs={{0,16},{16,32},{32,48},{48,64},{64,80},{80,96},{96,112},{1,17},{17... | collective-permute-start | bytes 786440 | tf_op jit(solution)/shard_map/ppermute | solution.py:13
  175.0 2.4 copy-start.6
  195.8 10.1 %copy-start.3 = (f32[4,32,8,5,64]{4,2,3,1,0:T(8,128)S(1)}, f32[4,32,8,5,64]{4,2,3,1,0:T(8,128)}, u32[]{:S(2)}) copy-start(f32[4,32,8,5,64]{4,2,3,1,0:T(8,128)} %get-tuple-element.18) | copy-start | bytes 3932164
  195.8 15.0 %all-to-all-start = ((bf16[8,2,16384]{2,1,0:T(2,128)(2,1)}), bf16[8,2,16384]{2,1,0:T(2,128)(2,1)S(1)}, u32[]{:S(2)}, u32[]{:S(2)}) async-start(bf16[8,2,16384]{2,1,0:T(2,128)(2,1)} %reshape.71), calls=%async_computation | async-start | bytes 1048576 | tf_op jit(solution)/shard_map/all_to_all | solution.py:71
  202.0 174.8 %all-gather.2.cloned.1.call-start = ((), (), s32[]{:S(2)}) async-start(), calls=%async_computation.3 | async-start | bytes 9437184 | tf_op jit(solution)/shard_map/all_gather | solution.py:77
  237.2 3.4 copy-start.5
  237.2 3.5 copy-start.7
  402.2 13.6 %copy-start.4 = (pred[8,6]{1,0:T(8,128)(4,1)S(1)}, pred[8,6]{1,0:T(8,128)(4,1)}, u32[]{:S(2)}) copy-start(pred[8,6]{1,0:T(8,128)(4,1)} %constant.31) | copy-start | bytes 148
  419.7 70.3 %all-to-all-start.1 = ((bf16[8,2,16384]{2,1,0:T(2,128)(2,1)}), bf16[8,2,16384]{2,1,0:T(2,128)(2,1)S(1)}, u32[]{:S(2)}, u32[]{:S(2)}) async-start(bf16[8,2,16384]{2,1,0:T(2,128)(2,1)} %reshape.73), calls=%async_computation.1 | async-start | bytes 1048576 | tf_op jit(solution)/shard_map/all_to_all | solution.py:80
  424.6 200.6 %all-reduce.5.cloned.1.call-start = ((), (), s32[]{:S(2)}) async-start(), calls=%async_computation.5 | async-start | bytes 221184 | tf_op jit(solution)/shard_map/psum | solution.py:84
  489.9 284.1 %all-reduce.3.cloned.1.call-start = ((), (), s32[]{:S(2)}) async-start(), calls=%async_computation.4 | async-start | bytes 884736 | tf_op jit(solution)/shard_map/psum | solution.py:83
  502.3 46.7 %copy-start.2 = (f32[16,16,8,3,128]{4,1,3,2,0:T(8,128)S(1)}, f32[16,16,8,3,128]{4,1,3,2,0:T(8,128)}, u32[]{:S(2)}) copy-start(f32[16,16,8,3,128]{4,1,3,2,0:T(8,128)} %copy.139) | copy-start | bytes 9437188
  548.9 278.3 %reduce-scatter.4.cloned.1.call-start = ((), (), s32[]{:S(2)}) async-start(), calls=%async_computation.6 | async-start | bytes 2359296
  625.2 206.2 %copy-start.1 = (bf16[3,3,3,32,64]{4,3,2,1,0:T(8,128)(2,1)S(1)}, bf16[3,3,3,32,64]{4,3,2,1,0:T(8,128)(2,1)}, u32[]{:S(2)}) copy-start(bf16[3,3,3,32,64]{4,3,2,1,0:T(8,128)(2,1)} %param.5) | copy-start | bytes 331780
Sparse Core Ops, SparseCore 0:
  206.0 170.6 all-gather.1
  490.1 135.0 all-reduce.4
  631.2 142.7 all-reduce.2
  776.3 50.8 reduce-scatter.3
where the time goes:
time: 853 us; the launch traced here: 838 us
  waiting for transfers between devices  343 us (40%)
  local copies, waits for them, and re-layouts  263 us (31%)
  matrix products  137 us (16%)
  other arithmetic  66 us (8%)
  starting transfers between devices  15.2 us (2%)
  between operations  14.4 us (2%)
    psum x1, waiting for transfers between devices, shards(): total_a = lax.psum(local_a, ('mp', 'dp'))  147 us
    transpose x2, matrix products, kernel_grad(): return jnp.transpose(result, (1, 2, 3, 0, 4))  98.3 us
    all_gather x1, waiting for transfers between devices, shards(): upstream = lax.all_gather(cotangent, 'mp', axis=4, tiled=True)  97.7 us
    unnamed x32, local copies, waits for them, and re-layouts  66.3 us
    concatenate x1, other arithmetic, shards(): padded_x = pad_sides(jnp.concatenate([below, field], axis=1))  58.2 us
    unnamed x5, waiting for transfers between devices  51.4 us
    psum x1, waiting for transfers between devices, shards(): total_b = lax.psum(local_b, 'dp')  45.1 us
    concatenate x2, local copies, waits for them, and re-layouts, shards(): padded_x = pad_sides(jnp.concatenate([below, field], axis=1))  39.5 us
  transfers between devices with their start and end apart: 7, of which 5 were waited for; matrix products, arithmetic and copies ran while one was open for 32% of the time, Pallas kernels for 0%

commit v1 on v0

--- a/solution.py
+++ b/solution.py
@@ -80,7 +80,7 @@
     back = lax.all_to_all(back_group, "mp", split_axis=1, concat_axis=4, tiled=True)
     delta = (back.astype(jnp.float32) * jnp.where(pre > 0, 1.0, 0.3)).astype(jnp.bfloat16)
     local_a = kernel_grad(padded_x, delta)
-    total_a = lax.psum(local_a, ("mp", "dp"))
+    total_a = lax.psum(lax.psum(local_a, "mp"), "dp")
     total_b = lax.psum(local_b, "dp")
     samples_all = samp_local * lax.axis_size("dp")
     grad_a = total_a / math.sqrt(samples_all * (GRID // 2) ** 3)

time: 853 us -> 685 us (0.80)
  waiting for transfers between devices: 343 us -> 174 us
    all_gather x1, waiting for transfers between devices: 97.7 us -> 0.01 us  [shards(): upstream = lax.all_gather(cotangent, 'mp', axis=4, tiled=True)]
    psum x2, waiting for transfers between devices: 192 us -> 122 us  [shards(): total_a = lax.psum(lax.psum(local_a, 'mp'), 'dp')]
    unnamed x32 -> x34, local copies, waits for them, and re-layouts: 66.3 us -> 66 us
  transfers between devices with their start and end apart: 7 -> 7, of which waited for: 5 -> 3; matrix products, arithmetic and copies ran while one was open for 32% -> 59% of each run, Pallas kernels for 0% -> 0%
where the time goes in v1:
time: 685 us; the launch traced here: 672 us
  local copies, waits for them, and re-layouts  265 us (39%)
  waiting for transfers between devices  174 us (25%)
  matrix products  138 us (20%)
  other arithmetic  66.1 us (10%)
  starting transfers between devices  15.3 us (2%)
  between operations  14.3 us (2%)
    psum x2, waiting for transfers between devices, shards(): total_a = lax.psum(lax.psum(local_a, 'mp'), 'dp')  122 us
    transpose x2, matrix products, kernel_grad(): return jnp.transpose(result, (1, 2, 3, 0, 4))  98.8 us
    unnamed x34, local copies, waits for them, and re-layouts  66 us
    concatenate x1, other arithmetic, shards(): padded_x = pad_sides(jnp.concatenate([below, field], axis=1))  58.2 us
    unnamed x5, waiting for transfers between devices  51.5 us
    concatenate x2, local copies, waits for them, and re-layouts, shards(): padded_x = pad_sides(jnp.concatenate([below, field], axis=1))  39.6 us
    conv_general_dilated x6, local copies, waits for them, and re-layouts, forward_conv(): lax.conv_general_dilated(padded, kernel, (2, 2, 2), 'VALID', dimension_nu...  37.1 us
    all_to_all x4, local copies, waits for them, and re-layouts, shards(): lax.all_to_all(hidden, 'mp', split_axis=4, concat_axis=1, tiled=True)  33.1 us
  transfers between devices with their start and end apart: 7, of which 3 were waited for; matrix products, arithmetic and copies ran while one was open for 59% of the time, Pallas kernels for 0%

profile of v1, /device:TPU:1, one launch (start us, length us, event | category | flops | bytes accessed | tf_op | source)
XLA Modules:
  0.0 671.9 jit_solution(3457501782090073605)
XLA Ops:
  7.2 4.9 copy.124
  13.2 1.1 copy.125
  14.3 4.0 collective-permute-start
  18.3 2.6 copy.140
  20.9 31.5 %copy.127 = bf16[1,8,64,64,32]{4,0,3,2,1:T(2,128)(2,1)} copy(bf16[1,8,64,64,32]{2,4,3,1,0:T(8,128)(2,1)} %bitcast.69) | data formatting | bytes 4194304 | tf_op jit(solution)/shard_map/reshape | solution.py:66
  52.3 2.7 copy.126
  55.0 58.2 %pad_maximum_fusion = bf16[1,9,64,64,32]{4,0,3,2,1:T(2,128)(2,1)} fusion(bf16[1,8,64,64,32]{4,0,3,2,1:T(2,128)(2,1)} %copy.127, bf16[1,1,64,64,32]{4,0,3,2,1:T(2,128)(2,1)S(1)} %copy.126), kind=kLoop, calls=%fused_computation.4 | loop fusion | flops 1179648 | bytes 4718592 | tf_op jit(solution)/shard_map/concatenate | solution.py:68
  113.2 33.5 %copy.128 = bf16[1,9,64,64,32]{3,4,2,1,0:T(8,128)(2,1)} copy(bf16[1,9,64,64,32]{4,0,3,2,1:T(2,128)(2,1)} %pad_maximum_fusion) | data formatting | bytes 4718592 | tf_op jit(solution)/shard_map/concatenate | solution.py:68
  146.7 9.2 %copy.159 = bf16[9,64,1,64,32]{1,4,3,0,2:T(8,128)(2,1)} copy(bf16[9,64,1,64,32]{3,4,2,1,0:T(8,128)(2,1)} %bitcast.72) | data formatting | bytes 4718592
  156.0 6.1 pad.4.clone
  162.0 15.6 %copy.131 = bf16[9,64,1,8,10,32]{5,3,4,1,0,2:T(8,128)(2,1)} copy(bf16[9,64,1,8,10,32]{1,5,4,3,0,2:T(8,128)(2,1)} %bitcast.67) | data formatting | bytes 5898240 | tf_op jit(solution)/shard_map/conv_general_dilated | solution.py:17
  177.7 2.3 slice.12
  180.1 12.0 %compare_select_fusion = (f32[4,32,8,5,64]{4,2,3,1,0:T(8,128)}, bf16[4,32,8,5,64]{4,2,3,1,0:T(8,128)(2,1)S(1)}) fusion(pred[8,5]{0,1:T(8,128)(4,1)S(1)} %copy-done.7, bf16[3,3,3,32,64]{4,3,2,1,0:T(8,128)(2,1)S(1)} %copy-done, bf16[9,64,1,7,2,32]{5,3,4,1,0,2:T(8,128)(2,1)S(1)} %slice.12, bf16[9,64,1,8,10,32]{5,3,4,1,0,2:T(8,128)(2,1)} %copy.131), kind=kOutput, calls=%fused_computation.20 | convolution fusion | flops 572915712 | bytes 5541928 | tf_op jit(solution)/shard_map/conv_general_dilated | solution.py:17
  192.5 3.4 copy.133
  195.9 2.7 reshape.71
  198.6 5.9 all-to-all-start
  204.5 10.0 %copy.141 = bf16[1,16,16,16,128]{4,3,2,1,0:T(8,128)(2,1)S(1)} copy(bf16[1,16,16,16,128]{3,2,1,0,4:T(8,128)(2,1)} %all-gather.2.cloned.1.call-done) | data formatting | bytes 2097152 | tf_op jit(solution)/shard_map/all_gather | solution.py:77
  215.7 14.0 %fusion.17 = bf16[32,32,8,6,8]{4,2,3,1,0:T(8,128)(2,1)} fusion(bf16[3,3,3,8,128]{4,3,2,1,0:T(8,128)(2,1)S(1)} %copy-done.5, bf16[16,16,1,7,1,128]{5,3,4,1,0,2:T(8,128)(2,1)S(1)} %slice.16, bf16[16,16,1,8,3,128]{5,3,4,1,0,2:T(8,128)(2,1)S(1)} %copy.144), kind=kOutput, calls=%fused_computation.24 | convolution fusion | flops 332021760 | bytes 2873344 | tf_op jit(solution)/shard_map/conv_general_dilated | solution.py:42
  229.7 13.6 %copy.145 = bf16[32,32,8,6,8]{1,4,3,2,0:T(8,128)(2,1)S(1)} copy(bf16[32,32,8,6,8]{4,2,3,1,0:T(8,128)(2,1)} %fusion.17) | data formatting | bytes 1572864 | tf_op jit(solution)/shard_map/conv_general_dilated | solution.py:42
  244.5 2.7 reshape.73
  247.2 5.1 all-to-all-start.1
  252.6 2.2 copy.149
  255.0 2.9 copy.158
  257.9 3.1 reshape.72
  260.9 2.9 copy.134
  263.8 2.2 copy.135
  266.0 3.4 copy.160
  269.4 4.0 pad.6.clone
  273.5 12.8 %copy.138 = bf16[32,32,1,8,6,8]{5,3,4,1,0,2:T(8,128)(2,1)} copy(bf16[32,32,1,8,6,8]{1,5,4,3,0,2:T(8,128)(2,1)} %bitcast.73) | data formatting | bytes 1572864 | tf_op jit(solution)/shard_map/conv_general_dilated | solution.py:17
  286.2 5.6 slice.14
  291.9 24.0 %copy.153 = bf16[1,32,32,32,8]{4,0,3,2,1:T(2,128)(2,1)} copy(bf16[1,32,32,32,8]{3,4,2,1,0:T(8,128)(2,1)S(1)} %bitcast.71) | data formatting | bytes 1048576 | tf_op jit(solution)/shard_map/all_to_all | solution.py:71
  315.9 14.3 %copy.154 = bf16[1,16,16,16,128]{4,0,3,2,1:T(2,128)(2,1)} copy(bf16[1,16,16,16,128]{3,2,1,0,4:T(8,128)(2,1)} %all-gather.2.cloned.1.call-done) | data formatting | bytes 2097152 | tf_op jit(solution)/shard_map/all_gather | solution.py:77
  331.2 3.4 copy.147
  334.6 3.5 fusion.12
  338.1 4.1 copy.151
  342.2 47.0 %fusion.35 = f32[3,3,3,32,64]{4,3,2,1,0:T(8,128)} fusion(bf16[1,9,64,64,32]{4,0,3,2,1:T(2,128)(2,1)} %pad_maximum_fusion, bf16[1,4,32,32,64]{4,0,3,2,1:T(2,128)(2,1)} %copy.151), kind=kOutput, calls=%fused_computation.45 | convolution fusion | flops 443596800 | bytes 3104768 | tf_op jit(solution)/shard_map/transpose | solution.py:37
  389.4 51.8 %fusion.36 = f32[3,3,3,8,128]{4,3,2,1,0:T(8,128)} fusion(bf16[1,32,32,32,8]{4,0,3,2,1:T(2,128)(2,1)} %copy.153, bf16[1,16,16,16,128]{4,0,3,2,1:T(2,128)(2,1)S(1)} %copy-done.2), kind=kOutput, calls=%fused_computation.46 | convolution fusion | flops 212629504 | bytes 1683456 | tf_op jit(solution)/shard_map/transpose | solution.py:37
  441.1 22.3 %all-reduce.4.cloned.1.call-done = f32[3,3,3,32,64]{4,3,2,1,0:T(8,128)} async-done(((f32[3,3,3,32,64]{4,3,2,1,0:T(8,128)}), f32[3,3,3,32,64]{4,3,2,1,0:T(8,128)}) %all-reduce.4.cloned.1.call-update) | async-done | bytes 221200 | tf_op jit(solution)/shard_map/psum | solution.py:83
  463.5 13.0 %broadcast_select_fusion = f32[16,16,8,3,128]{4,2,3,1,0:T(8,128)S(1)} fusion(pred[8,3]{0,1:T(4,128)(4,1)S(1)} %copy-done.8, bf16[3,3,3,8,128]{4,3,2,1,0:T(8,128)(2,1)S(1)} %copy-done.6, bf16[32,32,1,7,2,8]{5,3,4,1,0,2:T(8,128)(2,1)} %slice.14, bf16[32,32,1,8,6,8]{5,3,4,1,0,2:T(8,128)(2,1)} %copy.138), kind=kOutput, calls=%fused_computation.30 | convolution fusion | flops 329662464 | bytes 4216856 | tf_op jit(solution)/shard_map/conv_general_dilated | solution.py:17
  477.2 13.5 %copy.156 = f32[1,16,16,16,128]{2,3,1,0,4:T(8,128)} copy(f32[1,16,16,16,128]{4,2,3,1,0:T(8,128)S(1)} %slice_bitcast_fusion.1) | data formatting | bytes 4194304
  490.7 15.3 %reshape.69 = f32[128,4096]{1,0:T(8,128)} reshape(f32[128,1,16,16,16]{4,3,2,1,0:T(8,128)} %bitcast.66) | data formatting | bytes 4194304
  506.0 100.2 %all-reduce.6.cloned.1.call-done = (f32[3,3,3,32,64]{4,3,2,1,0:T(8,128)}, f32[3,3,3,8,128]{4,3,2,1,0:T(8,128)}) async-done(((f32[3,3,3,32,64]{4,3,2,1,0:T(8,128)}, f32[3,3,3,8,128]{4,3,2,1,0:T(8,128)}), (f32[3,3,3,32,64]{4,3,2,1,0:T(8,128)}, f32[3,3,3,8,128]{4,3,2,1,0:T(8,128)})) %all-reduce.6.cloned.1.call-update) | async-done | bytes 331792 | tf_op jit(solution)/shard_map/psum | solution.py:83
  606.2 1.5 broadcast_multiply_fusion.1
  607.7 1.9 broadcast_multiply_fusion
  609.6 51.4 %reduce-scatter.4.cloned.1.call-done = f32[16,4096]{1,0:T(8,128)} async-done(((f32[128,4096]{1,0:T(8,128)}), f32[16,4096]{1,0:T(8,128)}) %reduce-scatter.4.cloned.1.call-update) | async-done | bytes 262160
  661.0 1.7 reshape.70
  662.8 1.2 copy.157
  664.0 1.2 copy.155
  (43 shorter events, 6.2 us)
Async XLA Ops:
  7.2 172.9 %copy-start = (bf16[3,3,3,32,64]{4,3,2,1,0:T(8,128)(2,1)S(1)}, bf16[3,3,3,32,64]{4,3,2,1,0:T(8,128)(2,1)}, u32[]{:S(2)}) copy-start(bf16[3,3,3,32,64]{4,3,2,1,0:T(8,128)(2,1)} %param.5) | copy-start | bytes 331780
  7.2 11.1 %copy-start.3 = (bf16[1,16,16,16,16]{4,3,2,1,0:T(8,128)(2,1)S(1)}, bf16[1,16,16,16,16]{4,3,2,1,0:T(8,128)(2,1)}, u32[]{:S(2)}) copy-start(bf16[1,16,16,16,16]{4,3,2,1,0:T(8,128)(2,1)} %param.7) | copy-start | bytes 393220
  7.2 197.3 %all-gather.2.cloned.1.call-start = ((), (), s32[]{:S(2)}) async-start(), calls=%async_computation.3 | async-start | bytes 9437184 | tf_op jit(solution)/shard_map/all_gather | solution.py:77
  14.3 38.1 %collective-permute-start = (bf16[1,1,64,64,32]{3,4,2,1,0:T(8,128)(2,1)S(1)}, bf16[1,1,64,64,32]{3,4,2,1,0:T(8,128)(2,1)S(1)}, u32[]{:S(2)}, u32[]{:S(2)}) collective-permute-start(bf16[1,1,64,64,32]{3,4,2,1,0:T(8,128)(2,1)S(1)} %copy.125), channel_id=1, source_target_pairs={{0,16},{16,32},{32,48},{48,64},{64,80},{80,96},{96,112},{1,17},{17... | collective-permute-start | bytes 786440 | tf_op jit(solution)/shard_map/ppermute | solution.py:13
  177.7 2.4 copy-start.7
  198.6 48.6 %all-to-all-start = ((bf16[8,2,16384]{2,1,0:T(2,128)(2,1)}), bf16[8,2,16384]{2,1,0:T(2,128)(2,1)}, u32[]{:S(2)}, u32[]{:S(2)}) async-start(bf16[8,2,16384]{2,1,0:T(2,128)(2,1)} %reshape.71), calls=%async_computation | async-start | bytes 1048576 | tf_op jit(solution)/shard_map/all_to_all | solution.py:71
  214.8 0.9 copy-start.5
  229.7 13.6 %copy-start.4 = (pred[8,6]{1,0:T(8,128)(4,1)S(1)}, pred[8,6]{1,0:T(8,128)(4,1)}, u32[]{:S(2)}) copy-start(pred[8,6]{1,0:T(8,128)(4,1)} %constant.31) | copy-start | bytes 148
  247.2 83.0 %all-to-all-start.1 = ((bf16[8,2,16384]{2,1,0:T(2,128)(2,1)}), bf16[8,2,16384]{2,1,0:T(2,128)(2,1)S(1)}, u32[]{:S(2)}, u32[]{:S(2)}) async-start(bf16[8,2,16384]{2,1,0:T(2,128)(2,1)} %reshape.73), calls=%async_computation.1 | async-start | bytes 1048576 | tf_op jit(solution)/shard_map/all_to_all | solution.py:80
  252.3 211.1 %all-reduce.4.cloned.1.call-start = ((), (), s32[]{:S(2)}) async-start(), calls=%async_computation.4 | async-start | bytes 884736 | tf_op jit(solution)/shard_map/psum | solution.py:83
  342.2 47.1 %copy-start.2 = (bf16[1,16,16,16,128]{4,0,3,2,1:T(2,128)(2,1)S(1)}, bf16[1,16,16,16,128]{4,0,3,2,1:T(2,128)(2,1)}, u32[]{:S(2)}) copy-start(bf16[1,16,16,16,128]{4,0,3,2,1:T(2,128)(2,1)} %copy.154) | copy-start | bytes 3145732
  389.3 74.2 %copy-start.6 = (bf16[3,3,3,8,128]{4,3,2,1,0:T(8,128)(2,1)S(1)}, bf16[3,3,3,8,128]{4,3,2,1,0:T(8,128)(2,1)}, u32[]{:S(2)}) copy-start(bf16[3,3,3,8,128]{4,3,2,1,0:T(8,128)(2,1)} %param.6) | copy-start | bytes 165892
  389.3 74.2 %copy-start.8 = (pred[8,3]{0,1:T(4,128)(4,1)S(1)}, pred[8,3]{0,1:T(4,128)(4,1)}, u32[]{:S(2)}) copy-start(pred[8,3]{0,1:T(4,128)(4,1)} %constant.29) | copy-start | bytes 76
  389.3 216.9 %all-reduce.6.cloned.1.call-start = ((), (), s32[]{:S(2)}) async-start(), calls=%async_computation.6 | async-start | bytes 1105920 | tf_op jit(solution)/shard_map/psum | solution.py:83
  463.4 197.6 %reduce-scatter.4.cloned.1.call-start = ((), (), s32[]{:S(2)}) async-start(), calls=%async_computation.5 | async-start | bytes 2359296
  607.7 57.5 %copy-start.1 = (bf16[3,3,3,32,64]{4,3,2,1,0:T(8,128)(2,1)S(1)}, bf16[3,3,3,32,64]{4,3,2,1,0:T(8,128)(2,1)}, u32[]{:S(2)}) copy-start(bf16[3,3,3,32,64]{4,3,2,1,0:T(8,128)(2,1)} %param.5) | copy-start | bytes 331780
Sparse Core Ops, SparseCore 0:
  21.0 170.8 all-gather.1
  389.4 73.9 all-reduce.3
  466.7 139.4 all-reduce.5
  608.5 52.5 reduce-scatter.3
